TPU v7x, 32 devices: a whole 2x2x4 slice. The times are simulated.
32 devices in a mesh: groups: 2 (over y), uv: 4 (over z), tm: 2 (over x), chan: 2 (over core).
Axes of the slice: x: 2, y: 2, z: 4, core: 2. Of those that a mesh axis runs over, the one named last changes fastest.
Arguments:
- visibilities: bfloat16 [2, 4, 8192, 256], P(None, 'tm', ('groups', 'uv'), 'chan'), parts along dimension 2, may hold values from -6 to 6
- baseline_keep_mask: int32 [8192], P(('groups', 'uv')), parts along dimension 0, may hold values 0 or 1
- channel_flags: int32 [512], P(('groups', 'chan')), parts along dimension 0, may hold values 0 or 1
- baseline_spacing: float32 [2, 4, 8192], P(None, 'tm', ('groups', 'uv')), parts along dimension 2, may hold values from -200 to 200
- tile_owner: int32 [4, 8192, 1], P('tm', ('groups', 'uv')), parts along dimension 1, may hold values from 0 to 3; in each aligned block of 1024 rows (0 to 1023, 1024 to 2047, ..., all dimensions but the last counted through in order) at most 640 rows name the same one
- tile_cell_index: int32 [4, 8192], P('tm', ('groups', 'uv')), parts along dimension 1, may hold values from 0 to 1023
- directions: float32 [2, 1024], replicated, may hold values from -0.1 to 0.1
- sky_flux: bfloat16 [1024, 256], P(None, 'chan'), may hold values from -0.1875 to 0.1875
Outputs:
- residual: bfloat16 [2, 4, 8192, 256], P(None, 'tm', ('groups', 'uv'), 'chan'), parts along dimension 2
- dirty_grid: float32 [8, 2, 1024, 256], P(('groups', 'uv'), None, 'tm', 'chan'), parts along dimension 0
- gradient: float32 [2048, 256], P('groups', 'chan'), parts along dimension 0
There are 2 independent parts, one for each index of `groups`. A program takes and returns all parts, laid end to end along the dimension named above; an argument that names none is the same for every part. Nothing has to cross between parts.
Inputs may be any that keep to these rules, and one draw needn't show every extreme that they name: `tile_owner`: each aligned block of 1024 entries (one dump of the baselines of one index of uv) names any tile at most 640 times; in some blocks a tile is named exactly 640 times.
All inputs are finite; a program needn't handle non-finite values. No bound on the sum of `baseline_keep_mask` or of `channel_flags` on one device may be relied on, other than what follows from the above.
Results may differ from a plain program's by a relative error of at most 0.008.
Values may be sent and summed in bfloat16 or wider, within the bound.
A program may use at most 64 MiB of HBM per device.

v0:
```python
import math

import jax
import jax.numpy as jnp
from jax import lax
from jax.sharding import PartitionSpec as P

CELLS = 1024


TWO_PI = 2.0 * math.pi


def grid_rows(row_values, row_cells):
    slot_total = row_cells.shape[0]
    block_count = max(1, slot_total // 1024)
    while slot_total % block_count:
        block_count += 1
    block_width = slot_total // block_count
    cell_range = jnp.arange(CELLS, dtype=jnp.int32)
    initial = jnp.zeros((row_values.shape[0], row_values.shape[2], CELLS), jnp.float32)

    def grid_block(block_index, accumulated):
        start_slot = block_index * block_width
        value_rows_block = lax.dynamic_slice_in_dim(row_values, start_slot, block_width, 1)
        cells_block = lax.dynamic_slice_in_dim(row_cells, start_slot, block_width, 0)
        picker_mask = (cells_block[:, None] == cell_range[None, :]).astype(jnp.bfloat16)
        return accumulated + jnp.einsum(
            "rde,du->reu", value_rows_block, picker_mask, preferred_element_type=jnp.float32
        )

    summed = lax.fori_loop(0, block_count, grid_block, initial)
    return jnp.swapaxes(summed, 1, 2)


def spread_gradient(grad_share):
    summed_share = lax.psum(grad_share.astype(jnp.bfloat16), "uv").astype(jnp.float32)
    joined = lax.all_gather(summed_share, "tm", axis=1, tiled=True)
    return joined.reshape(joined.shape[0] * joined.shape[1], joined.shape[2])


def shards(
    visibilities,
    baseline_keep_mask,
    channel_flags,
    baseline_spacing,
    tile_owner,
    tile_cell_index,
    directions,
    sky_flux,
):
    dump_count = visibilities.shape[1]
    base_count = visibilities.shape[2]
    chan_width = visibilities.shape[3]
    row_count = dump_count * base_count
    owner_count = lax.axis_size("uv")
    time_count = lax.axis_size("tm")
    total_rows = row_count * owner_count * time_count
    observed = visibilities.reshape(2, row_count, chan_width)
    spacing = baseline_spacing.reshape(2, row_count)
    row_flags = (
        jnp.broadcast_to(baseline_keep_mask[None, :], (dump_count, base_count))
        .reshape(row_count)
        .astype(jnp.float32)
    )
    chan_flags = channel_flags.astype(jnp.float32)
    block_rows = math.gcd(row_count, 512)

    def predict_block(block_index, state):
        grad_sum, resid_buffer = state
        start_row = block_index * block_rows
        rows_spacing = lax.dynamic_slice_in_dim(spacing, start_row, block_rows, 1)
        turns = (
            rows_spacing[0][:, None] * directions[0][None, :]
            + rows_spacing[1][:, None] * directions[1][None, :]
        )
        angle = turns * TWO_PI
        stacked = jnp.concatenate(
            [jnp.cos(angle).astype(jnp.bfloat16), jnp.sin(angle).astype(jnp.bfloat16)], 0
        )
        model = jnp.dot(stacked, sky_flux, preferred_element_type=jnp.float32)
        model_real = model[:block_rows]
        model_imag = -model[block_rows:]
        seen = lax.dynamic_slice_in_dim(observed, start_row, block_rows, 1).astype(jnp.float32)
        weights = (
            lax.dynamic_slice_in_dim(row_flags, start_row, block_rows, 0)[:, None]
            * chan_flags[None, :]
        )
        resid_real = ((seen[0] - model_real) * weights).astype(jnp.bfloat16)
        resid_imag = ((seen[1] - model_imag) * weights).astype(jnp.bfloat16)
        resid_buffer = lax.dynamic_update_slice_in_dim(
            resid_buffer, jnp.stack([resid_real, resid_imag]), start_row, 1
        )
        right_side = jnp.concatenate([resid_real, -resid_imag], 0)
        grad_sum = grad_sum + lax.dot_general(
            stacked, right_side, (((0,), (0,)), ((), ())), preferred_element_type=jnp.float32
        )
        return (grad_sum, resid_buffer)

    initial = (
        jnp.zeros((directions.shape[1], chan_width), jnp.float32),
        jnp.zeros((2, row_count, chan_width), jnp.bfloat16),
    )
    partial_grad, residual_rows = lax.fori_loop(0, row_count // block_rows, predict_block, initial)
    owners = tile_owner.reshape(dump_count, base_count)
    most_rows = 5 * base_count // (2 * owner_count)
    bucket_count = dump_count * most_rows
    owner_range = jnp.arange(owner_count, dtype=jnp.int32)
    owner_labels = (owners[:, :, None] == owner_range[None, None, :]).astype(jnp.bfloat16)
    base_range = jnp.arange(base_count, dtype=jnp.int32)
    lower_ones = (base_range[:, None] >= base_range[None, :]).astype(jnp.bfloat16)
    running = jnp.einsum(
        "rs,dso->dro", lower_ones, owner_labels, preferred_element_type=jnp.float32
    )
    ranks = jnp.sum((running - 1.0) * owner_labels.astype(jnp.float32), axis=2).astype(jnp.int32)
    slot_keys = owners * most_rows + ranks
    slot_range = jnp.arange(owner_count * most_rows, dtype=jnp.int32).reshape(
        owner_count, most_rows
    )
    matches = slot_keys[:, None, None, :] == slot_range[None, :, :, None]
    picker = matches.astype(jnp.bfloat16)
    rows_by_dump = residual_rows.reshape(2, dump_count, base_count, chan_width)
    placed = jnp.einsum(
        "dokb,pdbf->podkf", picker, rows_by_dump, preferred_element_type=jnp.float32
    ).astype(jnp.bfloat16)
    send_rows = placed.reshape(2, owner_count * bucket_count, chan_width)
    cells_plus = tile_cell_index + 1
    placed_cells = jnp.sum(matches.astype(jnp.int32) * cells_plus[:, None, None, :], axis=3) - 1
    send_cells = jnp.transpose(placed_cells, (1, 0, 2)).reshape(owner_count * bucket_count)
    grad_parts = partial_grad.reshape(2, partial_grad.shape[0] // 2, chan_width)
    outgoing = send_rows.reshape(2, owner_count, bucket_count, chan_width)
    outgoing_cells = send_cells.reshape(1, owner_count, bucket_count)
    arrived, arrived_cells = (
        lax.all_to_all(outgoing, "uv", split_axis=1, concat_axis=1, tiled=True),
        lax.all_to_all(outgoing_cells, "uv", split_axis=1, concat_axis=1, tiled=True),
    )
    local_grid_sum = grid_rows(
        arrived.reshape(2, owner_count * bucket_count, chan_width),
        arrived_cells.reshape(owner_count * bucket_count),
    )
    grid_share, grad_share = (
        lax.psum_scatter(local_grid_sum, "tm", scatter_dimension=1, tiled=True),
        lax.psum_scatter(grad_parts, "tm", scatter_dimension=1, tiled=True),
    )
    total_grad = spread_gradient(grad_share)
    residual = residual_rows.reshape(2, dump_count, base_count, chan_width)
    dirty_grid = grid_share[None]
    gradient = -(total_grad / math.sqrt(total_rows))
    return (residual, dirty_grid, gradient)


def solution(mesh):
    placed = (
        P(None, "tm", ("groups", "uv"), "chan"),
        P(("groups", "uv")),
        P(("groups", "chan")),
        P(None, "tm", ("groups", "uv")),
        P("tm", ("groups", "uv"), None),
        P("tm", ("groups", "uv")),
        P(),
        P(None, "chan"),
    )
    return jax.shard_map(
        shards,
        mesh=mesh,
        in_specs=placed,
        out_specs=(
            P(None, "tm", ("groups", "uv"), "chan"),
            P(("groups", "uv"), None, "tm", "chan"),
            P("groups", "chan"),
        ),
        check_vma=False,
    )
```

profile of v0, /device:TPU:0, one launch (start us, length us, event | category | flops | bytes accessed | tf_op | source)
XLA Modules:
  0.0 216.6 jit_solution(14178345911820260646)
XLA Ops:
  9.4 59.2 %while.30 = (s32[]{:T(128)}, f32[1024,128]{1,0:T(8,128)}, bf16[2,2048,128]{2,1,0:T(8,128)(2,1)S(1)}, f32[2,2048]{1,0:T(2,128)S(1)}, f32[2,1024]{1,0:T(2,128)}, /...) while((s32[]{:T(128)}, f32[1024,128]{1,0:T(8,128)}, ...), condition=%wide.region_1.0_spmd.clone, body=%wide.region_0.0_spmd.clone.sunk | while | flops 550502400 | bytes 11187421 | solution.py:104
  10.3 8.5 %cosine_convert_fusion.2 = (bf16[512,1024]{1,0:T(8,128)(2,1)S(1)}, bf16[512,1024]{1,0:T(8,128)(2,1)S(1)}) fusion(f32[1024]{0:T(1024)S(1)} %bitcast.103, f32[512]{0:T(512)S(1)} %bitcast.105, f32[1024]{0:T(1024)S(1)} %bitcast.102, f32[512]{0:T(512)S(1)} %bitcast.104), kind=kLoop, calls=%fused_computation.3.clone.1 | loop fusion | flops 3145728 | bytes 2109440 | tf_op jit(solution)/shard_map/while/body/eval_jaxpr/convert_element_type | solution.py:79
  24.3 8.5 %cosine_convert_fusion.2 = (bf16[512,1024]{1,0:T(8,128)(2,1)S(1)}, bf16[512,1024]{1,0:T(8,128)(2,1)S(1)}) fusion(f32[1024]{0:T(1024)S(1)} %bitcast.103, f32[512]{0:T(512)S(1)} %bitcast.105, f32[1024]{0:T(1024)S(1)} %bitcast.102, f32[512]{0:T(512)S(1)} %bitcast.104), kind=kLoop, calls=%fused_computation.3.clone.1 | loop fusion | flops 3145728 | bytes 2109440 | tf_op jit(solution)/shard_map/while/body/eval_jaxpr/convert_element_type | solution.py:79
  36.0 2.6 %fusion.64 = f32[1024,128]{1,0:T(8,128)} fusion(bf16[512,1024]{1,0:T(8,128)(2,1)S(1)} %get-tuple-element.442, bf16[512,1024]{1,0:T(8,128)(2,1)S(1)} %get-tuple-element.443, f32[1024,128]{1,0:T(8,128)} %get-tuple-element.465, bf16[512,128]{1,0:T(8,128)(2,1)S(1)} %get-tuple-element.444, bf16[512,128]{1,0:T(8,128)(2,1)S(1)} %fusion.63, pred[]{:T(512)S(6)} %compare.6), kind=kOutput, calls=%fused_computation.7.clone.1 | convolution fusion | flops 273416192 | bytes 3407873 | tf_op jit(solution)/shard_map/while/body/eval_jaxpr/dot_general | solution.py:95
  39.4 8.5 %cosine_convert_fusion.2 = (bf16[512,1024]{1,0:T(8,128)(2,1)S(1)}, bf16[512,1024]{1,0:T(8,128)(2,1)S(1)}) fusion(f32[1024]{0:T(1024)S(1)} %bitcast.103, f32[512]{0:T(512)S(1)} %bitcast.105, f32[1024]{0:T(1024)S(1)} %bitcast.102, f32[512]{0:T(512)S(1)} %bitcast.104), kind=kLoop, calls=%fused_computation.3.clone.1 | loop fusion | flops 3145728 | bytes 2109440 | tf_op jit(solution)/shard_map/while/body/eval_jaxpr/convert_element_type | solution.py:79
  51.0 2.6 %fusion.64 = f32[1024,128]{1,0:T(8,128)} fusion(bf16[512,1024]{1,0:T(8,128)(2,1)S(1)} %get-tuple-element.442, bf16[512,1024]{1,0:T(8,128)(2,1)S(1)} %get-tuple-element.443, f32[1024,128]{1,0:T(8,128)} %get-tuple-element.465, bf16[512,128]{1,0:T(8,128)(2,1)S(1)} %get-tuple-element.444, bf16[512,128]{1,0:T(8,128)(2,1)S(1)} %fusion.63, pred[]{:T(512)S(6)} %compare.6), kind=kOutput, calls=%fused_computation.7.clone.1 | convolution fusion | flops 273416192 | bytes 3407873 | tf_op jit(solution)/shard_map/while/body/eval_jaxpr/dot_general | solution.py:95
  54.5 8.5 %cosine_convert_fusion.2 = (bf16[512,1024]{1,0:T(8,128)(2,1)S(1)}, bf16[512,1024]{1,0:T(8,128)(2,1)S(1)}) fusion(f32[1024]{0:T(1024)S(1)} %bitcast.103, f32[512]{0:T(512)S(1)} %bitcast.105, f32[1024]{0:T(1024)S(1)} %bitcast.102, f32[512]{0:T(512)S(1)} %bitcast.104), kind=kLoop, calls=%fused_computation.3.clone.1 | loop fusion | flops 3145728 | bytes 2109440 | tf_op jit(solution)/shard_map/while/body/eval_jaxpr/convert_element_type | solution.py:79
  66.1 2.6 %fusion.64 = f32[1024,128]{1,0:T(8,128)} fusion(bf16[512,1024]{1,0:T(8,128)(2,1)S(1)} %get-tuple-element.442, bf16[512,1024]{1,0:T(8,128)(2,1)S(1)} %get-tuple-element.443, f32[1024,128]{1,0:T(8,128)} %get-tuple-element.465, bf16[512,128]{1,0:T(8,128)(2,1)S(1)} %get-tuple-element.444, bf16[512,128]{1,0:T(8,128)(2,1)S(1)} %fusion.63, pred[]{:T(512)S(6)} %compare.6), kind=kOutput, calls=%fused_computation.7.clone.1 | convolution fusion | flops 273416192 | bytes 3407873 | tf_op jit(solution)/shard_map/while/body/eval_jaxpr/dot_general | solution.py:95
  69.6 6.2 %convert_bitcast_fusion = bf16[2,4,2,640,128]{3,4,1,0,2:T(8,128)(2,1)S(1)} fusion(s32[4,640]{1,0:T(4,128)S(1)} %multiply_add_fusion, s32[2,1024]{1,0:T(2,128)S(1)} %get-tuple-element.352, bf16[2,2,1024,128,1]{3,2,1,0,4:T(8,128)(2,1)} %bitcast.98), kind=kOutput, calls=%fused_computation.41 | convolution fusion | flops 2690908160 | bytes 3688448 | tf_op jit(solution)/shard_map/dokb,pdbf->podkf/dot_general | solution.py:123
  75.9 2.6 %copy.44 = bf16[2,4,2,640,128]{4,3,2,0,1:T(8,128)(2,1)} copy(bf16[2,4,2,640,128]{3,4,1,0,2:T(8,128)(2,1)S(1)} %convert_bitcast_fusion) | data formatting | bytes 5242880 | tf_op jit(solution)/shard_map/reshape;reshape | solution.py:131
  78.5 6.3 %all-to-all-start = ((bf16[2,4,1280,128]{3,2,0,1:T(8,128)(2,1)}), bf16[2,4,1280,128]{3,2,0,1:T(8,128)(2,1)S(1)}, u32[]{:S(2)}, u32[]{:S(2)}) async-start(bf16[2,4,1280,128]{3,2,0,1:T(8,128)(2,1)} %bitcast.94), calls=%async_computation | async-start | bytes 5242880 | tf_op jit(solution)/shard_map/all_to_all | solution.py:134
  85.5 2.2 %fusion.22 = s32[2,4,640]{2,1,0:T(4,128)S(1)} fusion(s32[2,1024]{1,0:T(2,128)S(1)} %get-tuple-element.353, s32[4,640]{1,0:T(4,128)S(1)} %multiply_add_fusion, s32[2,1024]{1,0:T(2,128)S(1)} %get-tuple-element.352), kind=kLoop, calls=%fused_computation.34 | loop fusion | flops 15723520 | bytes 47104 | tf_op jit(solution)/shard_map/reduce_sum | solution.py:128
  88.4 55.8 %all-to-all-done = bf16[2,4,1280,128]{3,2,0,1:T(8,128)(2,1)S(1)} async-done(((bf16[2,4,1280,128]{3,2,0,1:T(8,128)(2,1)}), bf16[2,4,1280,128]{3,2,0,1:T(8,128)(2,1)S(1)}, u32[]{:S(2)}, u32[]{:S(2)}) %all-to-all-start) | async-done | bytes 2621472 | tf_op jit(solution)/shard_map/all_to_all | solution.py:134
  144.2 3.3 %all-to-all-start.1 = ((s32[1,4,1280]{2,0,1:T(1,128)}), s32[1,4,1280]{2,0,1:T(1,128)S(1)}, u32[]{:S(2)}, u32[]{:S(2)}) async-start(s32[1,4,1280]{2,0,1:T(1,128)} %copy.37), calls=%async_computation.1 | async-start | bytes 40960 | tf_op jit(solution)/shard_map/all_to_all | solution.py:135
  153.1 15.9 %while.31 = (s32[]{:T(128)}, f32[2,128,1024]{2,1,0:T(8,128)}, bf16[2,5120,128]{2,1,0:T(8,128)(2,1)}, s32[5120]{0:T(1024)S(1)}, s32[]{:T(128)}, /*index=5*/s32[]{:T(128)}, s32[]{:T(128)}, s32[]{:T(128)}) while((s32[]{:T(128)}, f32[2,128,1024]{2,1,0:T(8,128)}, bf16[2,5120,128]{2,1,0:T(8,128)(2,1)}, s32[5120]{0:T(1024)S(1)}, ...), condition=%wide.region_5.0_spmd.clone, body=%wide.region_4.0_spmd.clone.sunk | while | flops 538443776 | bytes 2633877 | solution.py:32
  153.1 2.9 %fusion.67 = f32[2,128,1024]{2,1,0:T(8,128)} fusion(s32[1024]{0:T(1024)S(1)} %dynamic_slice.50, f32[2,128,1024]{2,1,0:T(8,128)} %get-tuple-element.501, bf16[2,5120,128]{2,1,0:T(8,128)(2,1)} %get-tuple-element.510, s32[]{:T(128)S(6)} %select_n.23, pred[]{:T(512)S(6)} %compare.7), kind=kOutput, calls=%fused_computation.29.clone.1 | convolution fusion | flops 538443776 | bytes 2625541 | tf_op jit(solution)/shard_map/while/body/eval_jaxpr/rde,du->reu/dot_general | solution.py:28
  156.0 3.2 %fusion.67 = f32[2,128,1024]{2,1,0:T(8,128)} fusion(s32[1024]{0:T(1024)S(1)} %dynamic_slice.50, f32[2,128,1024]{2,1,0:T(8,128)} %get-tuple-element.501, bf16[2,5120,128]{2,1,0:T(8,128)(2,1)} %get-tuple-element.510, s32[]{:T(128)S(6)} %select_n.23, pred[]{:T(512)S(6)} %compare.7), kind=kOutput, calls=%fused_computation.29.clone.1 | convolution fusion | flops 538443776 | bytes 2625541 | tf_op jit(solution)/shard_map/while/body/eval_jaxpr/rde,du->reu/dot_general | solution.py:28
  159.2 3.2 %fusion.67 = f32[2,128,1024]{2,1,0:T(8,128)} fusion(s32[1024]{0:T(1024)S(1)} %dynamic_slice.50, f32[2,128,1024]{2,1,0:T(8,128)} %get-tuple-element.501, bf16[2,5120,128]{2,1,0:T(8,128)(2,1)} %get-tuple-element.510, s32[]{:T(128)S(6)} %select_n.23, pred[]{:T(512)S(6)} %compare.7), kind=kOutput, calls=%fused_computation.29.clone.1 | convolution fusion | flops 538443776 | bytes 2625541 | tf_op jit(solution)/shard_map/while/body/eval_jaxpr/rde,du->reu/dot_general | solution.py:28
  162.5 3.3 %fusion.67 = f32[2,128,1024]{2,1,0:T(8,128)} fusion(s32[1024]{0:T(1024)S(1)} %dynamic_slice.50, f32[2,128,1024]{2,1,0:T(8,128)} %get-tuple-element.501, bf16[2,5120,128]{2,1,0:T(8,128)(2,1)} %get-tuple-element.510, s32[]{:T(128)S(6)} %select_n.23, pred[]{:T(512)S(6)} %compare.7), kind=kOutput, calls=%fused_computation.29.clone.1 | convolution fusion | flops 538443776 | bytes 2625541 | tf_op jit(solution)/shard_map/while/body/eval_jaxpr/rde,du->reu/dot_general | solution.py:28
  165.7 3.3 %fusion.67 = f32[2,128,1024]{2,1,0:T(8,128)} fusion(s32[1024]{0:T(1024)S(1)} %dynamic_slice.50, f32[2,128,1024]{2,1,0:T(8,128)} %get-tuple-element.501, bf16[2,5120,128]{2,1,0:T(8,128)(2,1)} %get-tuple-element.510, s32[]{:T(128)S(6)} %select_n.23, pred[]{:T(512)S(6)} %compare.7), kind=kOutput, calls=%fused_computation.29.clone.1 | convolution fusion | flops 538443776 | bytes 2625541 | tf_op jit(solution)/shard_map/while/body/eval_jaxpr/rde,du->reu/dot_general | solution.py:28
  169.0 2.5 %copy.39 = f32[2,128,1024]{1,2,0:T(8,128)} copy(f32[2,128,1024]{2,1,0:T(8,128)} %get-tuple-element.253) | data formatting | bytes 2097152 | tf_op jit(solution)/shard_map/while | solution.py:32
  171.6 15.7 %all-reduce.2.cloned.1.call-done = bf16[2,256,128]{2,1,0:T(8,128)(2,1)} async-done(((bf16[2,256,128]{2,1,0:T(8,128)(2,1)}), bf16[2,256,128]{2,1,0:T(8,128)(2,1)}) %all-reduce.2.cloned.1.call-update) | async-done | bytes 131088 | tf_op jit(solution)/shard_map/psum | solution.py:37
  188.2 7.0 %all_gather.3 = f32[2,512,128]{2,1,0:T(8,128)S(1)} all-gather(f32[2,256,128]{2,1,0:T(8,128)S(1)} %convert_element_type.85), channel_id=1, replica_groups=mesh['groups'=2,'uv'=4,'tm'=2,'chan'=2] {'tm'}, dimensions={1}, use_global_device_ids=true | all-gather | bytes 786432 | tf_op jit(solution)/shard_map/all_gather | solution.py:38
  196.1 14.0 %reduce-scatter.3.cloned.1.call-done = f32[2,512,128]{2,1,0:T(8,128)} async-done(((f32[2,1024,128]{2,1,0:T(8,128)}), f32[2,512,128]{2,1,0:T(8,128)}) %reduce-scatter.3.cloned.1.call-update) | async-done | bytes 524304 | tf_op jit(solution)/shard_map/reduce_scatter | solution.py:142
  (70 shorter events, 29.1 us)
Async XLA Ops:
  9.4 59.2 %copy-start.1 = (s32[2,1024,1]{1,2,0:T(1,128)S(1)}, s32[2,1024,1]{1,2,0:T(1,128)}, u32[]{:S(2)}) copy-start(s32[2,1024,1]{1,2,0:T(1,128)} %param.16) | copy-start | bytes 24580
  9.4 59.7 %copy-start.2 = (s32[2,1024]{1,0:T(2,128)S(1)}, s32[2,1024]{1,0:T(2,128)}, u32[]{:S(2)}) copy-start(s32[2,1024]{1,0:T(2,128)} %param.17) | copy-start | bytes 24580
  68.6 1.0 copy-start
  78.5 65.7 %all-to-all-start = ((bf16[2,4,1280,128]{3,2,0,1:T(8,128)(2,1)}), bf16[2,4,1280,128]{3,2,0,1:T(8,128)(2,1)S(1)}, u32[]{:S(2)}, u32[]{:S(2)}) async-start(bf16[2,4,1280,128]{3,2,0,1:T(8,128)(2,1)} %bitcast.94), calls=%async_computation | async-start | bytes 5242880 | tf_op jit(solution)/shard_map/all_to_all | solution.py:134
  84.8 62.8 %reduce-scatter.5.cloned.1.call-start = ((), (), s32[]{:S(2)}) async-start(), calls=%async_computation.5 | async-start | bytes 786432 | tf_op jit(solution)/shard_map/reduce_scatter | solution.py:143
  144.2 8.9 %all-to-all-start.1 = ((s32[1,4,1280]{2,0,1:T(1,128)}), s32[1,4,1280]{2,0,1:T(1,128)S(1)}, u32[]{:S(2)}, u32[]{:S(2)}) async-start(s32[1,4,1280]{2,0,1:T(1,128)} %copy.37), calls=%async_computation.1 | async-start | bytes 40960 | tf_op jit(solution)/shard_map/all_to_all | solution.py:135
  147.5 39.8 %all-reduce.2.cloned.1.call-start = ((), (), s32[]{:S(2)}) async-start(), calls=%async_computation.6 | async-start | bytes 262144 | tf_op jit(solution)/shard_map/psum | solution.py:37
  149.2 60.8 %reduce-scatter.3.cloned.1.call-start = ((), (), s32[]{:S(2)}) async-start(), calls=%async_computation.4 | async-start | bytes 1572864 | tf_op jit(solution)/shard_map/reduce_scatter | solution.py:142
Sparse Core Ops, SparseCore 0:
  88.4 16.0 reduce-scatter.4
  151.3 35.8 all-reduce.1
  190.1 19.9 reduce-scatter.2
where the time goes:
time: 218 us; the launch traced here: 217 us
  waiting for transfers between devices  88.4 us (41%)
  other arithmetic  46.3 us (21%)
  matrix products  38.6 us (18%)
  between operations  13.8 us (6%)
  local copies, waits for them, and re-layouts  12.6 us (6%)
  starting transfers between devices  9.66 us (4%)
  blocking collectives  7.05 us (3%)
    all_to_all x1, waiting for transfers between devices, shards(): lax.all_to_all(outgoing, 'uv', split_axis=1, concat_axis=1, tiled=True)  55.8 us
    convert_element_type x4, other arithmetic, predict_block(): jnp.cos(angle).astype(jnp.bfloat16)  34 us
    dot_general x5, matrix products, grid_block(): jnp.einsum('rde,du->reu', value_rows_block, picker_mask, preferred_elemen...  15.9 us
    psum x1, waiting for transfers between devices, spread_gradient(): lax.psum(grad_share.astype(jnp.bfloat16), 'uv').astype(jnp.float32)  15.7 us
    reduce_scatter x1, waiting for transfers between devices, shards(): lax.psum_scatter(local_grid_sum, 'tm', scatter_dimension=1, tiled=True)  14 us
    dot_general x4, matrix products, predict_block(): lax.dot_general(stacked, right_side, (((0,), (0,)), ((), ())), preferred_...  9.31 us
    all_gather x1, blocking collectives, spread_gradient(): joined = lax.all_gather(summed_share, 'tm', axis=1, tiled=True)  7.05 us
    dot_general x4, matrix products, predict_block(): model = jnp.dot(stacked, sky_flux, preferred_element_type=jnp.float32)  6.61 us
  transfers between devices with their start and end apart: 5, of which 4 were waited for; matrix products, arithmetic and copies ran while one was open for 12% of the time, Pallas kernels for 0%

commit v1 on v0

v1 whole, which is shorter than its diff:
```python
import functools
import math

import jax
import jax.numpy as jnp
from jax import lax
from jax.experimental import pallas as pl
from jax.experimental.pallas import tpu as pltpu
from jax.sharding import PartitionSpec as P

CELLS = 1024
MESH = pl.DeviceIdType.MESH

SINE = (4.442867833714977, -7.307441175438759, 3.594769894002402, -0.7843319733145079)
COSINE = (1.4142134962388915, -6.978850945949801, 5.739460314170848, -1.8835574375552104, 0.3106869568258822)


def horner(coefs, x):
    total = coefs[-1]
    for coef in coefs[-2::-1]:
        total = total * x + coef
    return total


def predict(
    spacing_ref, keep_ref, chan_ref, dirs_ref, flux_ref, seen_ref, resid_ref, grad_ref, waves, l_wide, m_wide
):
    comps = dirs_ref.shape[0]
    rows = spacing_ref.shape[1]

    @pl.when(pl.program_id(0) == 0)
    def _():
        grad_ref[...] = jnp.zeros_like(grad_ref)
        l_wide[...] = jnp.broadcast_to(dirs_ref[:, 0:1], l_wide.shape)
        m_wide[...] = jnp.broadcast_to(dirs_ref[:, 1:2], m_wide.shape)

    step = 16

    def some(index, carry):
        at = pl.ds(pl.multiple_of(index * step, step), step)
        l = l_wide[at, :]
        m = m_wide[at, :]
        for lane in range(0, rows, 128):
            u = spacing_ref[0:1, lane : lane + 128]
            v = spacing_ref[1:2, lane : lane + 128]
            turns = u * l + v * m
            x = turns - jnp.round(turns)
            square = x * x
            half_sine = horner(SINE, square) * x
            half_cosine = horner(COSINE, square)
            waves[at, lane : lane + 128] = (1.0 - half_sine * half_sine).astype(jnp.bfloat16)
            waves[at, rows + lane : rows + lane + 128] = (half_sine * half_cosine).astype(jnp.bfloat16)
        return carry

    lax.fori_loop(0, comps // step, some, 0, unroll=2)
    model = jnp.dot(flux_ref[...], waves[...], preferred_element_type=jnp.float32).T
    keep = jnp.broadcast_to(keep_ref[...], (chan_ref.shape[1], rows)).T
    weights = keep * chan_ref[...]
    real = ((seen_ref[0].astype(jnp.float32) - model[:rows]) * weights).astype(jnp.bfloat16)
    imag = ((seen_ref[1].astype(jnp.float32) + model[rows:]) * weights).astype(jnp.bfloat16)
    resid_ref[0] = real
    resid_ref[1] = imag
    grad_ref[...] += jnp.dot(
        waves[...], jnp.concatenate([real, -imag], 0), preferred_element_type=jnp.float32
    )


def exchange(
    n, times, scale,
    ids_ref, resid_ref, grad_ref, grid_ref, total_ref,
    rows_ref, out_x, in_x, out_z, in_z, gout_x, gin_x, gout_z, gin_z, joined, gsum,
    xs, xr, zs, zr, gxs, gxr, gzs, gzr, azs, azr, axs, axr,
):
    i = lax.axis_index("uv")
    j = lax.axis_index("tm")
    chans = resid_ref.shape[2]
    width = CELLS // times

    def uv(step):
        return lax.rem(i + 1 + step, n)

    def tm(step):
        return lax.rem(j + 1 + step, times)

    barrier = pltpu.get_barrier_semaphore()
    for d in range(times - 1):
        pl.semaphore_signal(barrier, inc=1, device_id={"tm": tm(d)}, device_id_type=MESH)
    for s in range(n - 1):
        pl.semaphore_signal(barrier, inc=1, device_id={"uv": uv(s)}, device_id_type=MESH)
    pl.semaphore_wait(barrier, times - 1 + n - 1)

    def remote(src, dst, send, recv, device):
        return pltpu.make_async_remote_copy(
            src_ref=src, dst_ref=dst, send_sem=send, recv_sem=recv, device_id=device, device_id_type=MESH
        )

    def grid_x(s, d):
        return remote(out_x.at[s, d], in_x.at[s, d], xs.at[s, d], xr.at[s, d], {"tm": tm(d)})

    def grid_z(s):
        return remote(out_z.at[s], in_z.at[s], zs.at[s], zr.at[s], {"uv": uv(s)})

    def grad_x(d):
        return remote(gout_x.at[d], gin_x.at[d], gxs.at[d], gxr.at[d], {"tm": tm(d)})

    def grad_z(s):
        return remote(gout_z.at[s], gin_z.at[s], gzs.at[s], gzr.at[s], {"uv": uv(s)})

    def join_z(s):
        return remote(joined.at[j, i], joined.at[j, i], azs.at[s], azr.at[s], {"uv": uv(s)})

    def join_x(d):
        return remote(joined.at[j], joined.at[j], axs.at[d], axr.at[d], {"tm": tm(d)})

    def loop(low, high, body):
        def wrapped(s, carry):
            body(s)
            return carry

        lax.fori_loop(low, high, wrapped, 0)

    for d in range(times - 1):
        gout_x[d] = grad_ref[tm(d)].astype(gout_x.dtype)
        grad_x(d).start()

    rows_ref[:, :chans] = resid_ref[0]
    rows_ref[:, chans:] = resid_ref[1]

    def picked(tile, part):
        wanted = ids_ref[...] - (tile * CELLS + part * width)
        bins = lax.broadcasted_iota(jnp.int32, (width, rows_ref.shape[0]), 0)
        picker = jnp.where(bins == wanted, 1.0, 0.0).astype(jnp.bfloat16)
        return jnp.dot(picker, rows_ref[...], preferred_element_type=jnp.float32)

    def send_part(s):
        for d in range(times - 1):
            out_x[s, d] = picked(uv(s), tm(d)).astype(jnp.bfloat16)
            grid_x(s, d).start()

    loop(0, n, send_part)

    total = grad_ref[j]
    for d in range(times - 1):
        grad_x(d).wait_recv()
        total = total + gin_x[d].astype(jnp.float32)
    gsum[...] = total

    def send_grad(s):
        gout_z[s] = gsum[uv(s)].astype(gout_z.dtype)
        grad_z(s).start()

    loop(0, n - 1, send_grad)

    def add_part(s):
        mine = picked(uv(s), j)
        for d in range(times - 1):
            grid_x(s, d).wait_recv()
            mine = mine + in_x[s, d].astype(jnp.float32)
        return mine

    def forward(s):
        out_z[s] = add_part(s).astype(jnp.bfloat16)
        grid_z(s).start()

    loop(0, 1, forward)
    gsum[0] = gsum[i]

    def add_grad(s):
        grad_z(s).wait_recv()
        gsum[0] = gsum[0] + gin_z[s].astype(jnp.float32)

    loop(0, n - 1, add_grad)
    joined[j, i] = gsum[0].astype(joined.dtype)
    loop(0, n - 1, lambda s: join_z(s).start())
    loop(1, n - 1, forward)

    def joined_from(s):
        sender = lax.rem(i + n - 1 - s, n)
        remote(joined.at[j, sender], joined.at[j, sender], azs.at[s], azr.at[s], {"uv": uv(s)}).wait_recv()

    loop(0, n - 1, joined_from)
    for d in range(times - 1):
        join_x(d).start()

    mine = add_part(n - 1)
    grid_ref[0] = mine[:, :chans]
    grid_ref[1] = mine[:, chans:]

    def add_tile(s):
        grid_z(s).wait_recv()
        arrived = in_z[s].astype(jnp.float32)
        grid_ref[0] += arrived[:, :chans]
        grid_ref[1] += arrived[:, chans:]

    loop(0, n - 1, add_tile)
    for d in range(times - 1):
        sender = lax.rem(j + times - 1 - d, times)
        remote(joined.at[sender], joined.at[sender], axs.at[d], axr.at[d], {"tm": tm(d)}).wait_recv()
    total_ref[...] = joined[...].astype(jnp.float32) * scale

    def sent_parts(s):
        for d in range(times - 1):
            grid_x(s, d).wait_send()

    def sent_rest(s):
        grad_z(s).wait_send()
        join_z(s).wait_send()
        grid_z(s).wait_send()

    loop(0, n, sent_parts)
    loop(0, n - 1, sent_rest)
    for d in range(times - 1):
        grad_x(d).wait_send()
        join_x(d).wait_send()


def shards(
    visibilities,
    baseline_keep_mask,
    channel_flags,
    baseline_spacing,
    tile_owner,
    tile_cell_index,
    directions,
    sky_flux,
):
    dumps, base, chans = visibilities.shape[1:]
    rows = dumps * base
    n = lax.axis_size("uv")
    times = lax.axis_size("tm")
    comps = directions.shape[1]
    block = math.gcd(base, 512)
    per_dump = base // block
    vmem = pltpu.CompilerParams(vmem_limit_bytes=48 << 20)
    resid, grad = pl.pallas_call(
        predict,
        grid=(rows // block,),
        in_specs=[
            pl.BlockSpec((2, block), lambda k: (0, k)),
            pl.BlockSpec((1, block), lambda k: (0, lax.rem(k, per_dump))),
            pl.BlockSpec((1, chans), lambda k: (0, 0)),
            pl.BlockSpec((comps, 2), lambda k: (0, 0)),
            pl.BlockSpec((chans, comps), lambda k: (0, 0)),
            pl.BlockSpec((2, block, chans), lambda k: (0, k, 0)),
        ],
        out_specs=[
            pl.BlockSpec((2, block, chans), lambda k: (0, k, 0)),
            pl.BlockSpec((comps, chans), lambda k: (0, 0)),
        ],
        out_shape=[
            jax.ShapeDtypeStruct((2, rows, chans), jnp.bfloat16),
            jax.ShapeDtypeStruct((comps, chans), jnp.float32),
        ],
        scratch_shapes=[
            pltpu.VMEM((comps, 2 * block), jnp.bfloat16),
            pltpu.VMEM((comps, 128), jnp.float32),
            pltpu.VMEM((comps, 128), jnp.float32),
        ],
        compiler_params=vmem,
        name="predict",
    )(
        baseline_spacing.reshape(2, rows),
        baseline_keep_mask.astype(jnp.float32).reshape(1, base),
        channel_flags.astype(jnp.float32).reshape(1, chans),
        directions.T,
        sky_flux.T,
        visibilities.reshape(2, rows, chans),
    )
    ids = tile_owner.reshape(1, rows) * CELLS + tile_cell_index.reshape(1, rows)
    width = CELLS // times
    piece = comps // (times * n)
    kind = jnp.bfloat16 if piece % 16 == 0 else jnp.float32
    dma = pltpu.SemaphoreType.DMA
    whole = pl.BlockSpec(memory_space=pltpu.VMEM)
    grid, total = pl.pallas_call(
        functools.partial(exchange, n, times, -1.0 / math.sqrt(rows * n * times)),
        in_specs=[whole] * 3,
        out_specs=[whole] * 2,
        out_shape=[
            jax.ShapeDtypeStruct((2, width, chans), jnp.float32),
            jax.ShapeDtypeStruct((times, n, piece, chans), jnp.float32),
        ],
        scratch_shapes=[
            pltpu.VMEM((rows, 2 * chans), jnp.bfloat16),
            pltpu.VMEM((n, times - 1, width, 2 * chans), jnp.bfloat16),
            pltpu.VMEM((n, times - 1, width, 2 * chans), jnp.bfloat16),
            pltpu.VMEM((n - 1, width, 2 * chans), jnp.bfloat16),
            pltpu.VMEM((n - 1, width, 2 * chans), jnp.bfloat16),
            pltpu.VMEM((times - 1, n, piece, chans), kind),
            pltpu.VMEM((times - 1, n, piece, chans), kind),
            pltpu.VMEM((n - 1, piece, chans), kind),
            pltpu.VMEM((n - 1, piece, chans), kind),
            pltpu.VMEM((times, n, piece, chans), kind),
            pltpu.VMEM((n, piece, chans), jnp.float32),
            dma((n, times - 1)),
            dma((n, times - 1)),
            dma((n - 1,)),
            dma((n - 1,)),
            dma((times - 1,)),
            dma((times - 1,)),
            dma((n - 1,)),
            dma((n - 1,)),
            dma((n - 1,)),
            dma((n - 1,)),
            dma((times - 1,)),
            dma((times - 1,)),
        ],
        compiler_params=pltpu.CompilerParams(
            collective_id=0, has_side_effects=True, vmem_limit_bytes=56 << 20
        ),
        name="exchange",
    )(ids, resid, grad.reshape(times, n, piece, chans))
    return (
        resid.reshape(2, dumps, base, chans),
        grid[None],
        total.reshape(comps, chans),
    )


def solution(mesh):
    placed = (
        P(None, "tm", ("groups", "uv"), "chan"),
        P(("groups", "uv")),
        P(("groups", "chan")),
        P(None, "tm", ("groups", "uv")),
        P("tm", ("groups", "uv"), None),
        P("tm", ("groups", "uv")),
        P(),
        P(None, "chan"),
    )
    return jax.shard_map(
        shards,
        mesh=mesh,
        in_specs=placed,
        out_specs=(
            P(None, "tm", ("groups", "uv"), "chan"),
            P(("groups", "uv"), None, "tm", "chan"),
            P("groups", "chan"),
        ),
        check_vma=False,
    )
```

time: 218 us -> 66.5 us (0.31)
  waiting for transfers between devices: 88.4 us -> 0 us
  Pallas kernels: 0 us -> 55.7 us
  other arithmetic: 46.3 us -> 2.05 us
  matrix products: 38.6 us -> 0 us
  between operations: 13.8 us -> 0.7 us
  starting transfers between devices: 9.66 us -> 0 us
  blocking collectives: 7.05 us -> 0 us
  local copies, waits for them, and re-layouts: 12.6 us -> 6.96 us
    all_to_all x2 -> x0, waiting for transfers between devices: 57.9 us -> none  [the longest x1 55.8 us: shards(): lax.all_to_all(outgoing, 'uv', split_axis=1, concat_axis=1, tiled=True)]
    pallas_call x0 -> x2, Pallas kernels: none -> 55.7 us  [the longest x1 41.7 us: shards(): pl.pallas_call(functools.partial(exchange, n, times, -1.0 / math.sqrt(row...]
    convert_element_type x16 -> x1, other arithmetic: 42.4 us -> 0.69 us  [shards(): baseline_keep_mask.astype(jnp.float32).reshape(1, base)]
    dot_general x15 -> x0, matrix products: 38.6 us -> none  [the longest x5 15.9 us: grid_block(): jnp.einsum('rde,du->reu', value_rows_block, picker_mask, preferred_elemen...]
    psum x1 -> x0, waiting for transfers between devices: 15.7 us -> none  [spread_gradient(): lax.psum(grad_share.astype(jnp.bfloat16), 'uv').astype(jnp.float32)]
    reduce_scatter x2 -> x0, waiting for transfers between devices: 14 us -> none  [the longest x1 14 us: shards(): lax.psum_scatter(local_grid_sum, 'tm', scatter_dimension=1, tiled=True)]
    all_to_all x2 -> x0, starting transfers between devices: 9.58 us -> none  [the longest x1 6.32 us: shards(): lax.all_to_all(outgoing, 'uv', split_axis=1, concat_axis=1, tiled=True)]
    all_gather x1 -> x0, blocking collectives: 7.05 us -> none  [spread_gradient(): joined = lax.all_gather(summed_share, 'tm', axis=1, tiled=True)]
  transfers between devices with their start and end apart: 5 -> 0, of which waited for: 4 -> 0; matrix products, arithmetic and copies ran while one was open for 12% -> 0% of each run, Pallas kernels for 0% -> 0%
where the time goes in v1:
time: 66.5 us; the launch traced here: 65.5 us
  Pallas kernels  55.7 us (84%)
  local copies, waits for them, and re-layouts  6.96 us (10%)
  other arithmetic  2.05 us (3%)
  between operations  0.7 us (1%)
    pallas_call x1, Pallas kernels, shards(): pl.pallas_call(functools.partial(exchange, n, times, -1.0 / math.sqrt(row...  41.7 us
    pallas_call x1, Pallas kernels, shards(): pl.pallas_call(predict, grid=(rows // block,), in_specs=[pl.BlockSpec((2,...  14.1 us
    unnamed x14, local copies, waits for them, and re-layouts  6.96 us

profile of v1, /device:TPU:0, one launch (start us, length us, event | category | flops | bytes accessed | tf_op | source)
XLA Modules:
  0.0 65.5 jit_solution(7971335299761231309)
XLA Ops:
  0.6 0.0 copy-start.3
  0.6 0.0 copy-start
  0.7 0.7 %convert_bitcast_fusion.chan_ref = f32[1,128]{1,0:T(1,128)S(1)} fusion(s32[128]{0:T(128)} %param.10), kind=kLoop, calls=%fused_computation.1 | loop fusion | flops 128 | bytes 1024 | tf_op jit(solution)/shard_map/reshape | solution.py:264
  1.4 0.7 %convert_element_type.6 = f32[1024]{0:T(1024)S(1)} convert(s32[1024]{0:T(1024)} %param.9) | non-fusion elementwise | flops 1024 | bytes 8192 | tf_op jit(solution)/shard_map/convert_element_type | solution.py:263
  2.1 0.0 copy-done.3
  2.1 0.7 %copy.14 = s32[1,1,2,1024]{3,1,2,0:T(1,128)S(1)} copy(s32[1,1,2,1024]{3,2,1,0:T(2,128)} %bitcast.28) | data formatting | bytes 16384
  2.8 0.6 add.3.ids_ref
  3.4 0.7 %copy.13 = f32[1,2,2,1024]{3,1,2,0:T(2,128)S(1)} copy(f32[1,2,2,1024]{3,2,1,0:T(2,128)} %bitcast.27) | data formatting | bytes 32768
  4.2 1.1 %copy.12 = bf16[1024,128]{0,1:T(8,128)(2,1)S(1)} copy(bf16[1024,128]{1,0:T(8,128)(2,1)} %param.15) | data formatting | bytes 524288 | tf_op args[7]
  5.2 0.9 %copy.11 = f32[2,1024]{0,1:T(8,128)S(1)} copy(f32[2,1024]{1,0:T(2,128)} %param.14) | data formatting | bytes 16384 | tf_op args[6]
  6.2 0.0 copy-done
  6.2 14.1 %predict.1 = (bf16[2,2048,128]{2,1,0:T(8,128)(2,1)}, f32[1024,128]{1,0:T(8,128)S(1)}) custom-call(f32[2,2048]{1,0:T(2,128)S(1)} %bitcast.20, f32[1,1024]{1,0:T(1,128)S(1)} %bitcast.21, f32[1,128]{1,0:T(1,128)S(1)} %convert_bitcast_fusion.chan_ref, f32[1024,2]{1,0:T(8,128)S(1)} %bitcast.16, bf16[128,1024]{1,0:T(8,128)(2,1)S(1)} %bitcast.18, ...), custom_call_target="tpu_custom_call" | custom-call | tf_op jit(solution)/shard_map/predict/pallas_call | solution.py:235
  20.3 0.0 copy-start.1
  20.3 0.8 %copy-done.1 = f32[1024,128]{1,0:T(8,128)} copy-done((f32[1024,128]{1,0:T(8,128)}, f32[1024,128]{1,0:T(8,128)S(1)}, u32[]{:S(2)}) %copy-start.1) | copy-done | bytes 524312
  21.1 41.7 %exchange.1 = (f32[2,512,128]{2,1,0:T(8,128)}, f32[2,4,128,128]{3,2,1,0:T(8,128)}) custom-call(s32[1,2048]{1,0:T(1,128)} %add.3.ids_ref, bf16[2,2048,128]{2,1,0:T(8,128)(2,1)} %get-tuple-element.7.resid_ref, f32[2,4,128,128]{3,2,1,0:T(8,128)} %bitcast.19), custom_call_target="tpu_custom_call" | custom-call | tf_op jit(solution)/shard_map/exchange/pallas_call | solution.py:275
  62.7 0.0 copy-start.2
  62.7 1.9 %copy.17 = f32[1,2,512,128]{3,2,1,0:T(8,128)} copy(f32[1,2,512,128]{3,2,1,0:T(8,128)} %bitcast.24) | data formatting | bytes 1048576
  64.7 0.0 copy-done.2
  64.7 0.8 %copy.18 = f32[1024,128]{1,0:T(8,128)} copy(f32[1024,128]{1,0:T(8,128)S(1)} %bitcast.23) | data formatting | bytes 1048576
  (1 shorter events, 0.0 us)
Async XLA Ops:
  0.6 1.5 %copy-start.3 = (s32[2,1024,1]{1,2,0:T(1,128)S(1)}, s32[2,1024,1]{1,2,0:T(1,128)}, u32[]{:S(2)}) copy-start(s32[2,1024,1]{1,2,0:T(1,128)} %param.12) | copy-start | bytes 24580
  0.6 5.5 %copy-start = (bf16[2,2,1024,128]{3,2,1,0:T(8,128)(2,1)S(1)}, bf16[2,2,1024,128]{3,2,1,0:T(8,128)(2,1)}, u32[]{:S(2)}) copy-start(bf16[2,2,1024,128]{3,2,1,0:T(8,128)(2,1)} %param.8) | copy-start | bytes 3145732
  20.3 0.8 %copy-start.1 = (f32[1024,128]{1,0:T(8,128)}, f32[1024,128]{1,0:T(8,128)S(1)}, u32[]{:S(2)}) copy-start(f32[1024,128]{1,0:T(8,128)S(1)} %get-tuple-element.8) | copy-start | bytes 1572868
  62.7 1.9 %copy-start.2 = (f32[2,4,128,128]{3,2,1,0:T(8,128)S(1)}, f32[2,4,128,128]{3,2,1,0:T(8,128)}, u32[]{:S(2)}) copy-start(f32[2,4,128,128]{3,2,1,0:T(8,128)} %get-tuple-element.10) | copy-start | bytes 1572868

commit v2 on v1

v2 whole, which is shorter than its diff:
```python
import functools
import math

import jax
import jax.numpy as jnp
from jax import lax
from jax.experimental import pallas as pl
from jax.experimental.pallas import tpu as pltpu
from jax.sharding import PartitionSpec as P

CELLS = 1024
MESH = pl.DeviceIdType.MESH
ROUNDER = 12582912.0

SINE = (4.442867833714977, -7.307441175438759, 3.594769894002402, -0.7843319733145079)
COSINE = (1.4142134962388915, -6.978850945949801, 5.739460314170848, -1.8835574375552104, 0.3106869568258822)


def horner(coefs, x):
    total = coefs[-1]
    for coef in coefs[-2::-1]:
        total = total * x + coef
    return total


def predict(
    spacing_ref, keep_ref, chan_ref, dirs_ref, flux_ref, seen_ref, resid_ref, grad_ref,
    waves, l_wide, m_wide, flux_turned, spacing,
):
    comps = dirs_ref.shape[1]
    rows = seen_ref.shape[1]
    base = spacing_ref.shape[2]
    chans = flux_ref.shape[1]
    block = pl.program_id(0)
    dump = lax.div(block * rows, base)
    first = lax.rem(block * rows, base)

    @pl.when(block == 0)
    def _():
        grad_ref[...] = jnp.zeros_like(grad_ref)
        l_wide[...] = jnp.broadcast_to(dirs_ref[0:1, :], (128, comps)).T
        m_wide[...] = jnp.broadcast_to(dirs_ref[1:2, :], (128, comps)).T
        flux_turned[...] = flux_ref[...].astype(jnp.float32).T.astype(jnp.bfloat16)

    here = pl.ds(pl.multiple_of(first, 128), rows)
    for axis in range(2):
        row = spacing_ref[axis, 0:1, here]
        for d in range(1, spacing_ref.shape[1]):
            row = jnp.where(dump == d, spacing_ref[axis, d : d + 1, here], row)
        spacing[axis : axis + 1, :] = row
    step = 16

    def some(index, carry):
        at = pl.ds(pl.multiple_of(index * step, step), step)
        l = l_wide[at, :]
        m = m_wide[at, :]
        for lane in range(0, rows, 128):
            u = spacing[0:1, lane : lane + 128]
            v = spacing[1:2, lane : lane + 128]
            turns = u * l + v * m
            x = turns - ((turns + ROUNDER) - ROUNDER)
            square = x * x
            half_sine = horner(SINE, square) * x
            half_cosine = horner(COSINE, square)
            waves[at, lane : lane + 128] = (1.0 - half_sine * half_sine).astype(jnp.bfloat16)
            waves[at, rows + lane : rows + lane + 128] = (half_sine * half_cosine).astype(jnp.bfloat16)
        return carry

    lax.fori_loop(0, comps // step, some, 0, unroll=2)
    model = jnp.dot(flux_turned[...], waves[...], preferred_element_type=jnp.float32).T
    keep_row = keep_ref[:, here].astype(jnp.float32)
    weights = jnp.broadcast_to(keep_row, (chans, rows)).T * chan_ref[...].astype(jnp.float32)
    real = ((seen_ref[0].astype(jnp.float32) - model[:rows]) * weights).astype(jnp.bfloat16)
    imag = ((seen_ref[1].astype(jnp.float32) + model[rows:]) * weights).astype(jnp.bfloat16)
    resid_ref[0] = real
    resid_ref[1] = imag
    grad_ref[...] += jnp.dot(
        waves[...], jnp.concatenate([real, -imag], 0), preferred_element_type=jnp.float32
    )


def exchange(
    n, times, scale,
    owner_ref, cell_ref, resid_ref, grad_ref, grid_ref, total_ref,
    ids_ref, rows_ref, out_x, in_x, out_z, in_z, gout_z, gin_z, shares, joined, part_sum,
    xs, xr, zs, zr, gxs, gxr, gzs, gzr, azs, azr,
):
    i = lax.axis_index("uv")
    j = lax.axis_index("tm")
    chans = resid_ref.shape[2]
    width = CELLS // times

    def uv(step):
        return lax.rem(i + 1 + step, n)

    def tm(step):
        return lax.rem(j + 1 + step, times)

    barrier = pltpu.get_barrier_semaphore()
    for d in range(times - 1):
        pl.semaphore_signal(barrier, inc=1, device_id={"tm": tm(d)}, device_id_type=MESH)
    for s in range(n - 1):
        pl.semaphore_signal(barrier, inc=1, device_id={"uv": uv(s)}, device_id_type=MESH)
    pl.semaphore_wait(barrier, times - 1 + n - 1)

    def remote(src, dst, send, recv, device):
        return pltpu.make_async_remote_copy(
            src_ref=src, dst_ref=dst, send_sem=send, recv_sem=recv, device_id=device, device_id_type=MESH
        )

    def grid_x(s, d):
        return remote(out_x.at[s, d], in_x.at[s, d], xs.at[s, d], xr.at[s, d], {"tm": tm(d)})

    more = jnp.maximum(i, n - 1 - i) - jnp.minimum(i, n - 1 - i)

    def tile_of(s):
        turn = jnp.maximum(s - more, 0)
        far = jnp.where(s < more, jnp.maximum(i, n - 1 - i) - s, jnp.minimum(i, n - 1 - i) - turn // 2)
        upward = jnp.where(s < more, 2 * i < n - 1, turn % 2 == 0)
        return jnp.where(upward, i + far, i - far)

    def arrival(way, tile):
        return remote(out_z.at[0], in_z.at[way, tile], zs.at[0], zr.at[way, tile], {"uv": uv(0)})

    def grid_z(s):
        tile = tile_of(s)
        way = jnp.where(tile > i, 0, 1)
        to = jnp.where(tile > i, i + 1, i - 1)
        return remote(out_z.at[s], in_z.at[way, tile], zs.at[s], zr.at[way, tile], {"uv": to})

    def grad_x(d, slot):
        return remote(shares.at[slot], shares.at[slot], gxs.at[d], gxr.at[d], {"tm": tm(d)})

    def grad_z(s):
        return remote(gout_z.at[s], gin_z.at[s], gzs.at[s], gzr.at[s], {"uv": uv(s)})

    def join_z(s, slot):
        return remote(joined.at[slot], joined.at[slot], azs.at[s], azr.at[s], {"uv": uv(s)})

    def loop(low, high, body):
        def wrapped(s, carry):
            body(s)
            return carry

        lax.fori_loop(low, high, wrapped, 0)

    def send_grad(s):
        gout_z[s] = grad_ref[uv(s)].astype(gout_z.dtype)
        grad_z(s).start()

    loop(0, n - 1, send_grad)
    base = owner_ref.shape[1]
    for d in range(owner_ref.shape[0]):
        ids_ref[:, d * base : (d + 1) * base] = owner_ref[d : d + 1, :] * CELLS + cell_ref[d : d + 1, :]
    rows_ref[:, :chans] = resid_ref[0]
    rows_ref[:, chans:] = resid_ref[1]

    def picked(tile, part):
        wanted = ids_ref[...] - (tile * CELLS + part * width)
        bins = lax.broadcasted_iota(jnp.int32, (width, rows_ref.shape[0]), 0)
        picker = jnp.where(bins == wanted, 1.0, 0.0).astype(jnp.bfloat16)
        return jnp.dot(picker, rows_ref[...], preferred_element_type=jnp.float32)

    def send_part(s):
        for d in range(times - 1):
            out_x[s, d] = picked(tile_of(s), tm(d)).astype(jnp.bfloat16)
            grid_x(s, d).start()

    loop(0, n // 2, send_part)
    share = grad_ref[i]
    for s in range(n - 1):
        grad_z(s).wait_recv()
        share = share + gin_z[s].astype(jnp.float32)
    shares[j] = share.astype(shares.dtype)
    for d in range(times - 1):
        grad_x(d, j).start()
    loop(n // 2, n, send_part)

    def add_part(s):
        mine = picked(tile_of(s), j)
        for d in range(times - 1):
            grid_x(s, d).wait_recv()
            mine = mine + in_x[s, d].astype(jnp.float32)
        part_sum[...] = mine

    def add_arrival(way, tile):
        arrival(way, tile).wait_recv()
        part_sum[...] += in_z[way, tile].astype(jnp.float32)

    def forward(s):
        add_part(s)
        tile = tile_of(s)

        @pl.when((tile > i) & (i > 0))
        def _():
            add_arrival(0, tile)

        @pl.when((tile < i) & (i < n - 1))
        def _():
            add_arrival(1, tile)

        out_z[s] = part_sum[...].astype(jnp.bfloat16)
        grid_z(s).start()

    loop(0, n - 2, forward)
    for d in range(times - 1):
        grad_x(d, lax.rem(j + times - 1 - d, times)).wait_recv()
    joined[i] = functools.reduce(
        lambda total, t: total + shares[t].astype(jnp.float32),
        range(1, times),
        shares[0].astype(jnp.float32),
    ).astype(joined.dtype)
    loop(0, n - 1, lambda s: join_z(s, i).start())
    loop(n - 2, n - 1, forward)
    add_part(n - 1)

    @pl.when(i > 0)
    def _():
        add_arrival(0, i)

    @pl.when(i < n - 1)
    def _():
        add_arrival(1, i)

    grid_ref[0] = part_sum[:, :chans]
    grid_ref[1] = part_sum[:, chans:]
    loop(0, n - 1, lambda s: join_z(s, lax.rem(i + n - 1 - s, n)).wait_recv())
    total_ref[...] = joined[...].astype(jnp.float32) * scale

    def sent_parts(s):
        for d in range(times - 1):
            grid_x(s, d).wait_send()

    def sent_rest(s):
        grad_z(s).wait_send()
        join_z(s, i).wait_send()
        grid_z(s).wait_send()

    loop(0, n, sent_parts)
    loop(0, n - 1, sent_rest)
    for d in range(times - 1):
        grad_x(d, j).wait_send()


def shards(
    visibilities,
    baseline_keep_mask,
    channel_flags,
    baseline_spacing,
    tile_owner,
    tile_cell_index,
    directions,
    sky_flux,
):
    dumps, base, chans = visibilities.shape[1:]
    rows = dumps * base
    n = lax.axis_size("uv")
    times = lax.axis_size("tm")
    comps = directions.shape[1]
    block = math.gcd(base, 512)
    vmem = pltpu.CompilerParams(vmem_limit_bytes=60 << 20)
    resid, grad = pl.pallas_call(
        predict,
        grid=(rows // block,),
        in_specs=[
            pl.BlockSpec((2, dumps, base), lambda k: (0, 0, 0)),
            pl.BlockSpec((1, base), lambda k: (0, 0)),
            pl.BlockSpec((1, chans), lambda k: (0, 0)),
            pl.BlockSpec((2, comps), lambda k: (0, 0)),
            pl.BlockSpec((comps, chans), lambda k: (0, 0)),
            pl.BlockSpec((2, block, chans), lambda k: (0, k, 0)),
        ],
        out_specs=[
            pl.BlockSpec((2, block, chans), lambda k: (0, k, 0)),
            pl.BlockSpec((comps, chans), lambda k: (0, 0)),
        ],
        out_shape=[
            jax.ShapeDtypeStruct((2, rows, chans), jnp.bfloat16),
            jax.ShapeDtypeStruct((comps, chans), jnp.float32),
        ],
        scratch_shapes=[
            pltpu.VMEM((comps, 2 * block), jnp.bfloat16),
            pltpu.VMEM((comps, 128), jnp.float32),
            pltpu.VMEM((comps, 128), jnp.float32),
            pltpu.VMEM((chans, comps), jnp.bfloat16),
            pltpu.VMEM((2, block), jnp.float32),
        ],
        compiler_params=vmem,
        name="predict",
    )(
        baseline_spacing,
        baseline_keep_mask.reshape(1, base),
        channel_flags.reshape(1, chans),
        directions,
        sky_flux,
        visibilities.reshape(2, rows, chans),
    )
    width = CELLS // times
    piece = comps // n
    kind = jnp.bfloat16 if piece % 16 == 0 else jnp.float32
    dma = pltpu.SemaphoreType.DMA
    whole = pl.BlockSpec(memory_space=pltpu.VMEM)
    grid, total = pl.pallas_call(
        functools.partial(exchange, n, times, -1.0 / math.sqrt(rows * n * times)),
        in_specs=[whole] * 4,
        out_specs=[whole] * 2,
        out_shape=[
            jax.ShapeDtypeStruct((2, width, chans), jnp.float32),
            jax.ShapeDtypeStruct((n, piece, chans), jnp.float32),
        ],
        scratch_shapes=[
            pltpu.VMEM((1, rows), jnp.int32),
            pltpu.VMEM((rows, 2 * chans), jnp.bfloat16),
            pltpu.VMEM((n, times - 1, width, 2 * chans), jnp.bfloat16),
            pltpu.VMEM((n, times - 1, width, 2 * chans), jnp.bfloat16),
            pltpu.VMEM((n - 1, width, 2 * chans), jnp.bfloat16),
            pltpu.VMEM((2, n, width, 2 * chans), jnp.bfloat16),
            pltpu.VMEM((n - 1, piece, chans), kind),
            pltpu.VMEM((n - 1, piece, chans), kind),
            pltpu.VMEM((times, piece, chans), kind),
            pltpu.VMEM((n, piece, chans), kind),
            pltpu.VMEM((width, 2 * chans), jnp.float32),
            dma((n, times - 1)),
            dma((n, times - 1)),
            dma((n - 1,)),
            dma((2, n)),
            dma((times - 1,)),
            dma((times - 1,)),
            dma((n - 1,)),
            dma((n - 1,)),
            dma((n - 1,)),
            dma((n - 1,)),
        ],
        compiler_params=pltpu.CompilerParams(
            collective_id=0, has_side_effects=True, vmem_limit_bytes=56 << 20
        ),
        name="exchange",
    )(tile_owner.reshape(dumps, base), tile_cell_index, resid, grad.reshape(n, piece, chans))
    return (
        resid.reshape(2, dumps, base, chans),
        grid[None],
        total.reshape(comps, chans),
    )


def solution(mesh):
    placed = (
        P(None, "tm", ("groups", "uv"), "chan"),
        P(("groups", "uv")),
        P(("groups", "chan")),
        P(None, "tm", ("groups", "uv")),
        P("tm", ("groups", "uv"), None),
        P("tm", ("groups", "uv")),
        P(),
        P(None, "chan"),
    )
    return jax.shard_map(
        shards,
        mesh=mesh,
        in_specs=placed,
        out_specs=(
            P(None, "tm", ("groups", "uv"), "chan"),
            P(("groups", "uv"), None, "tm", "chan"),
            P("groups", "chan"),
        ),
        check_vma=False,
    )
```

time: 66.5 us -> 61.1 us (0.919); the launches traced: 65.5 us -> 60.9 us
  local copies, waits for them, and re-layouts: 6.96 us -> 4.02 us
  other arithmetic: 2.05 us -> 0 us
    unnamed x14 -> x5, local copies, waits for them, and re-layouts: 6.96 us -> 4.02 us
    pallas_call x1, Pallas kernels: 14.1 us -> 15.9 us  [shards(): pl.pallas_call(predict, grid=(rows // block,), in_specs=[pl.BlockSpec((2,...]
    pallas_call x1, Pallas kernels: 41.7 us -> 40.4 us  [shards(): pl.pallas_call(functools.partial(exchange, n, times, -1.0 / math.sqrt(row...]
    reshape x1 -> x0, other arithmetic: 0.75 us -> none  [shards(): channel_flags.astype(jnp.float32).reshape(1, chans)]
    convert_element_type x1 -> x0, other arithmetic: 0.69 us -> none  [shards(): baseline_keep_mask.astype(jnp.float32).reshape(1, base)]
where the time goes in v2:
time: 61.1 us; the launch traced here: 60.9 us
  Pallas kernels  56.2 us (92%)
  local copies, waits for them, and re-layouts  4.02 us (7%)
  between operations  0.65 us (1%)
    pallas_call x1, Pallas kernels, shards(): pl.pallas_call(functools.partial(exchange, n, times, -1.0 / math.sqrt(row...  40.4 us
    pallas_call x1, Pallas kernels, shards(): pl.pallas_call(predict, grid=(rows // block,), in_specs=[pl.BlockSpec((2,...  15.9 us
    unnamed x5, local copies, waits for them, and re-layouts  4.02 us

profile of v2, /device:TPU:0, one launch (start us, length us, event | category | flops | bytes accessed | tf_op | source)
XLA Modules:
  0.0 60.9 jit_solution(8382341105879705118)
XLA Ops:
  0.6 1.3 %copy.13 = s32[2,1024,1]{1,0,2:T(2,128)} copy(s32[2,1024,1]{1,2,0:T(1,128)} %param.12) | data formatting | bytes 16384
  1.9 15.9 %predict.1 = (bf16[2,2048,128]{2,1,0:T(8,128)(2,1)}, f32[1024,128]{1,0:T(8,128)}) custom-call(f32[2,2,1024]{2,1,0:T(2,128)} %spacing_ref.1, s32[1,1024]{1,0:T(1,128)} %bitcast.16, s32[1,128]{1,0:T(1,128)} %bitcast.17, f32[2,1024]{1,0:T(2,128)} %dirs_ref.1, bf16[1024,128]{1,0:T(8,128)(2,1)} %flux_ref.1, bf16[2,2048,128]{2,1,0:T(8,128)(2,1)} %bitcast.10), custom_call_target="tpu_custom_call" | custom-call | tf_op jit(solution)/shard_map/predict/pallas_call | solution.py:262
  17.8 40.4 %exchange.1 = (f32[2,512,128]{2,1,0:T(8,128)}, f32[4,256,128]{2,1,0:T(8,128)}) custom-call(s32[2,1024]{1,0:T(2,128)} %bitcast.15, s32[2,1024]{1,0:T(2,128)} %cell_ref.1, bf16[2,2048,128]{2,1,0:T(8,128)(2,1)} %get-tuple-element.7.resid_ref, f32[4,256,128]{2,1,0:T(8,128)} %bitcast.12), custom_call_target="tpu_custom_call" | custom-call | tf_op jit(solution)/shard_map/exchange/pallas_call | solution.py:303
  58.2 0.0 copy-start
  58.2 1.9 %copy.16 = f32[1,2,512,128]{3,2,1,0:T(8,128)} copy(f32[1,2,512,128]{3,2,1,0:T(8,128)} %bitcast.14) | data formatting | bytes 1048576
  60.1 0.0 copy-done
  60.1 0.8 %copy.17 = f32[1024,128]{1,0:T(8,128)} copy(f32[1024,128]{1,0:T(8,128)S(1)} %bitcast.13) | data formatting | bytes 1048576
Async XLA Ops:
  58.2 1.9 %copy-start = (f32[4,256,128]{2,1,0:T(8,128)S(1)}, f32[4,256,128]{2,1,0:T(8,128)}, u32[]{:S(2)}) copy-start(f32[4,256,128]{2,1,0:T(8,128)} %get-tuple-element.10) | copy-start | bytes 1572868

commit v3 on v2

--- a/solution.py
+++ b/solution.py
@@ -66,7 +66,7 @@
             waves[at, rows + lane : rows + lane + 128] = (half_sine * half_cosine).astype(jnp.bfloat16)
         return carry
 
-    lax.fori_loop(0, comps // step, some, 0, unroll=2)
+    lax.fori_loop(0, comps // step, some, 0, unroll=8)
     model = jnp.dot(flux_turned[...], waves[...], preferred_element_type=jnp.float32).T
     keep_row = keep_ref[:, here].astype(jnp.float32)
     weights = jnp.broadcast_to(keep_row, (chans, rows)).T * chan_ref[...].astype(jnp.float32)
@@ -80,7 +80,7 @@
 
 
 def exchange(
-    n, times, scale,
+    n, times,
     owner_ref, cell_ref, resid_ref, grad_ref, grid_ref, total_ref,
     ids_ref, rows_ref, out_x, in_x, out_z, in_z, gout_z, gin_z, shares, joined, part_sum,
     xs, xr, zs, zr, gxs, gxr, gzs, gzr, azs, azr,
@@ -225,7 +225,7 @@
     grid_ref[0] = part_sum[:, :chans]
     grid_ref[1] = part_sum[:, chans:]
     loop(0, n - 1, lambda s: join_z(s, lax.rem(i + n - 1 - s, n)).wait_recv())
-    total_ref[...] = joined[...].astype(jnp.float32) * scale
+    total_ref[...] = joined[...]
 
     def sent_parts(s):
         for d in range(times - 1):
@@ -301,12 +301,12 @@
     dma = pltpu.SemaphoreType.DMA
     whole = pl.BlockSpec(memory_space=pltpu.VMEM)
     grid, total = pl.pallas_call(
-        functools.partial(exchange, n, times, -1.0 / math.sqrt(rows * n * times)),
+        functools.partial(exchange, n, times),
         in_specs=[whole] * 4,
         out_specs=[whole] * 2,
         out_shape=[
             jax.ShapeDtypeStruct((2, width, chans), jnp.float32),
-            jax.ShapeDtypeStruct((n, piece, chans), jnp.float32),
+            jax.ShapeDtypeStruct((n, piece, chans), kind),
         ],
         scratch_shapes=[
             pltpu.VMEM((1, rows), jnp.int32),
@@ -339,7 +339,7 @@
     return (
         resid.reshape(2, dumps, base, chans),
         grid[None],
-        total.reshape(comps, chans),
+        total.reshape(comps, chans).astype(jnp.float32) * (-1.0 / math.sqrt(rows * n * times)),
     )
 
 

time: 61.1 us -> 60.6 us (level)
  local copies, waits for them, and re-layouts: 4.02 us -> 2.1 us
  other arithmetic: 0 us -> 1.84 us
    unnamed x5 -> x4, local copies, waits for them, and re-layouts: 4.02 us -> 2.1 us
    mul x0 -> x1, other arithmetic: none -> 1.84 us  [shards(): total.reshape(comps, chans).astype(jnp.float32)]
where the time goes in v3:
time: 60.6 us; the launch traced here: 60.4 us
  Pallas kernels  55.8 us (92%)
  local copies, waits for them, and re-layouts  2.1 us (3%)
  other arithmetic  1.84 us (3%)
  between operations  0.65 us (1%)
    pallas_call x1, Pallas kernels, shards(): pl.pallas_call(functools.partial(exchange, n, times), in_specs=[whole] *...  40.3 us
    pallas_call x1, Pallas kernels, shards(): pl.pallas_call(predict, grid=(rows // block,), in_specs=[pl.BlockSpec((2,...  15.5 us
    unnamed x4, local copies, waits for them, and re-layouts  2.1 us
    mul x1, other arithmetic, shards(): total.reshape(comps, chans).astype(jnp.float32)  1.84 us

profile of v3, /device:TPU:0, one launch (start us, length us, event | category | flops | bytes accessed | tf_op | source)
XLA Modules:
  0.0 60.4 jit_solution(4328891617128813759)
XLA Ops:
  0.6 1.3 %copy.13 = s32[2,1024,1]{1,0,2:T(2,128)} copy(s32[2,1024,1]{1,2,0:T(1,128)} %param.12) | data formatting | bytes 16384
  1.9 15.5 %predict.1 = (bf16[2,2048,128]{2,1,0:T(8,128)(2,1)}, f32[1024,128]{1,0:T(8,128)}) custom-call(f32[2,2,1024]{2,1,0:T(2,128)} %spacing_ref.1, s32[1,1024]{1,0:T(1,128)} %bitcast.16, s32[1,128]{1,0:T(1,128)} %bitcast.17, f32[2,1024]{1,0:T(2,128)} %dirs_ref.1, bf16[1024,128]{1,0:T(8,128)(2,1)} %flux_ref.1, bf16[2,2048,128]{2,1,0:T(8,128)(2,1)} %bitcast.10), custom_call_target="tpu_custom_call" | custom-call | tf_op jit(solution)/shard_map/predict/pallas_call | solution.py:262
  17.4 40.3 %exchange.1 = (f32[2,512,128]{2,1,0:T(8,128)}, bf16[4,256,128]{2,1,0:T(8,128)(2,1)}) custom-call(s32[2,1024]{1,0:T(2,128)} %bitcast.15, s32[2,1024]{1,0:T(2,128)} %cell_ref.1, bf16[2,2048,128]{2,1,0:T(8,128)(2,1)} %get-tuple-element.7.resid_ref, f32[4,256,128]{2,1,0:T(8,128)} %bitcast.12), custom_call_target="tpu_custom_call" | custom-call | tf_op jit(solution)/shard_map/exchange/pallas_call | solution.py:303
  57.7 0.0 copy-start
  57.7 1.8 %convert_multiply_fusion = f32[4,256,128]{2,1,0:T(8,128)} fusion(bf16[4,256,128]{2,1,0:T(8,128)(2,1)} %get-tuple-element.10), kind=kLoop, calls=%fused_computation | loop fusion | flops 262144 | bytes 786432 | tf_op jit(solution)/shard_map/mul | solution.py:342
  59.6 0.0 copy-done
  59.6 0.8 %copy.15 = f32[1,2,512,128]{3,2,1,0:T(8,128)} copy(f32[1,2,512,128]{3,2,1,0:T(8,128)S(1)} %bitcast.14) | data formatting | bytes 1048576
Async XLA Ops:
  57.7 1.8 %copy-start = (f32[2,512,128]{2,1,0:T(8,128)S(1)}, f32[2,512,128]{2,1,0:T(8,128)}, u32[]{:S(2)}) copy-start(f32[2,512,128]{2,1,0:T(8,128)} %get-tuple-element.9) | copy-start | bytes 1572868
